TPU v7x, 32 devices: a whole 2x2x4 slice. The times are simulated.
32 devices in a mesh: dp: 8 (over z, x), mp: 4 (over y, core).
Axes of the slice: x: 2, y: 2, z: 4, core: 2. Of those that a mesh axis runs over, the one named last changes fastest.
Arguments:
- queries: bfloat16 [128, 80, 8192], P('dp', None, 'mp'), may hold values from -1.5 to 1.5
- response_keys: bfloat16 [128, 80, 1024], P('dp', None, 'mp'), may hold values from -1.5 to 1.5
- response_values: bfloat16 [128, 80, 1024], P('dp', None, 'mp'), may hold values from -6 to 6
- output_gradient: bfloat16 [128, 80, 8192], P('dp', None, 'mp'), may hold values from -16 to 16
- prompt_token_keys: bfloat16 [8, 256, 1024], P('dp', None, 'mp'), may hold values from -1.5 to 1.5
- prompt_token_values: bfloat16 [8, 256, 1024], P('dp', None, 'mp'), may hold values from -6 to 6
- normed_hidden_input: bfloat16 [128, 80, 5120], P('dp', None, 'mp'), may hold values from -6 to 6
- adapter_down_factor: bfloat16 [5120, 32], P('mp'), may hold values from -0.078125 to 0.078125
- adapter_up_factor: bfloat16 [32, 8192], P(None, 'mp'), may hold values from -0.0625 to 0.0625
- response_prompt_index: int32 [128], P('dp'), may hold values from 0 to 7, as said below
- response_lengths: int32 [128], P('dp'), may hold values from 1 to 80, as said below
Outputs:
- query_grad: bfloat16 [128, 80, 8192], P('dp', None, 'mp')
- response_key_gradient: bfloat16 [128, 80, 1024], P('dp', None, 'mp')
- response_value_gradient: bfloat16 [128, 80, 1024], P('dp', None, 'mp')
- prompt_key_grad: bfloat16 [8, 256, 1024], P('dp', None, 'mp')
- prompt_value_grad: bfloat16 [8, 256, 1024], P('dp', None, 'mp')
- down_factor_gradient: float32 [5120, 32], P('mp')
- up_factor_gradient: float32 [32, 8192], P(None, 'mp')
Inputs may be any that keep to these rules, and one draw needn't show every extreme that they name: `response_prompt_index`: responses 16 * d to 16 * d + 15 are those held by index d of dp, and prompt p is held by index p. Every prompt is named by exactly 16 responses; the responses of one index of dp come from exactly 4 prompts, 4 from each. `response_lengths`: among the 16 responses of each index of dp at least one has length 80.
All inputs are finite; a program needn't handle non-finite values.
Results may differ from a plain program's by a relative error of at most 0.017.
Values may be sent and summed in bfloat16 or wider, within the bound.
A program may use at most 128 MiB of HBM per device.

v0:
```python
import math

import jax
import jax.numpy as jnp
from jax import lax
from jax.sharding import PartitionSpec as P

QUERY_HEAD_COUNT = 64
KEY_VALUE_HEADS = 8
HEAD_SIZE = 128
GROUP = 16
SHARE = 4


adapter_scale = 2.0


def respond(query_rows, key_own, value_own, grad_rows, key_prompt, value_prompt, length):
    row_count = query_rows.shape[0]
    kv_heads = key_own.shape[1] // HEAD_SIZE
    query_group_width = QUERY_HEAD_COUNT // KEY_VALUE_HEADS
    prompt_count = key_prompt.shape[0]
    score_scale = 1.0 / math.sqrt(HEAD_SIZE)
    query_heads = query_rows.reshape(row_count, kv_heads, query_group_width, HEAD_SIZE)
    keys_front = key_prompt.reshape(prompt_count, kv_heads, HEAD_SIZE)
    values_front = value_prompt.reshape(prompt_count, kv_heads, HEAD_SIZE)
    keys_self = key_own.reshape(row_count, kv_heads, HEAD_SIZE)
    values_self = value_own.reshape(row_count, kv_heads, HEAD_SIZE)
    front_scores = (
        jnp.einsum("lgcd,mgd->gclm", query_heads, keys_front, preferred_element_type=jnp.float32)
        * score_scale
    )
    self_scores = (
        jnp.einsum("lgcd,mgd->gclm", query_heads, keys_self, preferred_element_type=jnp.float32)
        * score_scale
    )
    column = jnp.arange(row_count, dtype=jnp.int32)[None, :]
    position = jnp.arange(row_count, dtype=jnp.int32)[:, None]
    visible = (column <= position) & (column < length)
    denominator = jnp.sum(jnp.exp(front_scores), axis=-1, keepdims=True) + jnp.sum(
        jnp.where(visible, jnp.exp(self_scores), 0.0), axis=-1, keepdims=True
    )
    log_total = jnp.log(denominator)
    front_weights = jnp.exp(front_scores - log_total)
    self_weights = jnp.where(visible, jnp.exp(self_scores - log_total), 0.0)
    front_low = front_weights.astype(jnp.bfloat16)
    self_low = self_weights.astype(jnp.bfloat16)
    live = (jnp.arange(row_count, dtype=jnp.int32) < length)[:, None, None, None]
    grad_heads = grad_rows.reshape(row_count, kv_heads, query_group_width, HEAD_SIZE)
    grad_live = jnp.where(live, grad_heads, jnp.zeros_like(grad_heads))
    output = jnp.einsum(
        "gclm,mgd->lgcd", front_low, values_front, preferred_element_type=jnp.float32
    ) + jnp.einsum("gclm,mgd->lgcd", self_low, values_self, preferred_element_type=jnp.float32)
    row_dot = jnp.transpose(jnp.sum(grad_live.astype(jnp.float32) * output, axis=-1), (1, 2, 0))[
        ..., None
    ]
    front_wgrad = jnp.einsum(
        "lgcd,mgd->gclm", grad_live, values_front, preferred_element_type=jnp.float32
    )
    self_wgrad = jnp.einsum(
        "lgcd,mgd->gclm", grad_live, values_self, preferred_element_type=jnp.float32
    )
    front_sgrad = (front_weights * (front_wgrad - row_dot)).astype(jnp.bfloat16)
    self_sgrad = (self_weights * (self_wgrad - row_dot)).astype(jnp.bfloat16)
    query_part = (
        jnp.einsum("gclm,mgd->lgcd", front_sgrad, keys_front, preferred_element_type=jnp.float32)
        + jnp.einsum("gclm,mgd->lgcd", self_sgrad, keys_self, preferred_element_type=jnp.float32)
    ) * score_scale
    key_front = (
        jnp.einsum("gclm,lgcd->mgd", front_sgrad, query_heads, preferred_element_type=jnp.float32)
        * score_scale
    )
    key_self = (
        jnp.einsum("gclm,lgcd->mgd", self_sgrad, query_heads, preferred_element_type=jnp.float32)
        * score_scale
    )
    value_front_part = jnp.einsum(
        "gclm,lgcd->mgd", front_low, grad_live, preferred_element_type=jnp.float32
    )
    value_self_part = jnp.einsum(
        "gclm,lgcd->mgd", self_low, grad_live, preferred_element_type=jnp.float32
    )
    return (
        query_part.reshape(row_count, -1).astype(jnp.bfloat16),
        key_self.reshape(row_count, -1).astype(jnp.bfloat16),
        value_self_part.reshape(row_count, -1).astype(jnp.bfloat16),
        key_front.reshape(prompt_count, -1),
        value_front_part.reshape(prompt_count, -1),
    )


def shards(
    queries,
    response_keys,
    response_values,
    output_gradient,
    prompt_token_keys,
    prompt_token_values,
    normed_hidden_input,
    adapter_down_factor,
    adapter_up_factor,
    response_prompt_index,
    response_lengths,
):
    holders = lax.axis_size("dp")
    blocks = GROUP // SHARE
    flattened_hidden = normed_hidden_input.reshape(-1, normed_hidden_input.shape[2])
    inner_piece = jnp.dot(flattened_hidden, adapter_down_factor, preferred_element_type=jnp.float32)
    inner_sum = lax.psum(inner_piece.astype(jnp.bfloat16), "mp")
    source_keys, source_values = (
        lax.all_gather(prompt_token_keys, "dp", axis=0, tiled=True),
        lax.all_gather(prompt_token_values, "dp", axis=0, tiled=True),
    )

    def batched(array):
        return array.reshape((blocks, SHARE) + array.shape[1:])

    def one_block(items):
        query_rows, key_own, value_own, grad_rows, owners, lengths = items
        key_prompt = jnp.take(source_keys, owners, axis=0)
        value_prompt = jnp.take(source_values, owners, axis=0)
        return jax.vmap(respond)(
            query_rows, key_own, value_own, grad_rows, key_prompt, value_prompt, lengths
        )

    results = lax.map(
        one_block,
        (
            batched(queries),
            batched(response_keys),
            batched(response_values),
            batched(output_gradient),
            batched(response_prompt_index),
            batched(response_lengths),
        ),
    )
    query_grad, response_key_gradient, response_value_gradient, key_parts, value_parts = (
        jax.tree.map(lambda array: array.reshape((GROUP,) + array.shape[2:]), results)
    )
    owner_table = (
        jnp.arange(holders, dtype=jnp.int32)[:, None] == response_prompt_index[None, :]
    ).astype(jnp.float32)
    key_buffer = jnp.einsum(
        "nr,rpk->npk",
        owner_table,
        key_parts,
        precision=lax.Precision.HIGHEST,
        preferred_element_type=jnp.float32,
    )
    value_buffer = jnp.einsum(
        "nr,rpk->npk",
        owner_table,
        value_parts,
        precision=lax.Precision.HIGHEST,
        preferred_element_type=jnp.float32,
    )
    summed_keys, summed_values = (
        lax.psum_scatter(
            key_buffer.astype(jnp.bfloat16), "dp", scatter_dimension=0, tiled=True
        ).astype(jnp.float32),
        lax.psum_scatter(
            value_buffer.astype(jnp.bfloat16), "dp", scatter_dimension=0, tiled=True
        ).astype(jnp.float32),
    )
    flattened_gradient = query_grad.reshape(-1, query_grad.shape[2])
    backward_piece = jnp.einsum(
        "ql,ul->qu", flattened_gradient, adapter_up_factor, preferred_element_type=jnp.float32
    )
    back_sum = lax.psum(backward_piece.astype(jnp.bfloat16), "mp")
    adapter_product = adapter_scale / math.sqrt(flattened_gradient.shape[0] * lax.axis_size("dp"))
    up_term = (
        jnp.einsum("tr,tk->rk", inner_sum, flattened_gradient, preferred_element_type=jnp.float32)
        * adapter_product
    )
    down_term = (
        jnp.einsum("td,tr->dr", flattened_hidden, back_sum, preferred_element_type=jnp.float32)
        * adapter_product
    )
    down_factor_gradient, up_factor_gradient = (
        lax.psum(down_term.astype(jnp.bfloat16), "dp").astype(jnp.float32),
        lax.psum(up_term.astype(jnp.bfloat16), "dp").astype(jnp.float32),
    )
    return (
        query_grad,
        response_key_gradient,
        response_value_gradient,
        summed_keys.astype(jnp.bfloat16),
        summed_values.astype(jnp.bfloat16),
        down_factor_gradient,
        up_factor_gradient,
    )


def solution(mesh):
    placed = (
        P("dp", None, "mp"),
        P("dp", None, "mp"),
        P("dp", None, "mp"),
        P("dp", None, "mp"),
        P("dp", None, "mp"),
        P("dp", None, "mp"),
        P("dp", None, "mp"),
        P("mp", None),
        P(None, "mp"),
        P("dp"),
        P("dp"),
    )
    return jax.shard_map(
        shards,
        mesh=mesh,
        in_specs=placed,
        out_specs=(
            P("dp", None, "mp"),
            P("dp", None, "mp"),
            P("dp", None, "mp"),
            P("dp", None, "mp"),
            P("dp", None, "mp"),
            P("mp", None),
            P(None, "mp"),
        ),
        check_vma=False,
    )
```

profile of v0, /device:TPU:0, one launch (start us, length us, event | category | flops | bytes accessed | tf_op | source)
XLA Modules:
  0.0 617.0 jit_solution(12732367560518508234)
XLA Ops:
  10.2 2.6 convolution_convert_fusion
  12.8 40.2 %all-gather.3.cloned.1.call-done = bf16[8,256,256]{2,1,0:T(8,128)(2,1)} async-done(((bf16[1,256,256]{2,1,0:T(8,128)(2,1)}), bf16[8,256,256]{2,1,0:T(8,128)(2,1)}) %all-gather.3.cloned.1.call-update) | async-done | bytes 1048592 | tf_op jit(solution)/shard_map/all_gather | solution.py:111
  53.0 41.1 %all-gather.5.cloned.1.call-done = bf16[8,256,256]{2,1,0:T(8,128)(2,1)} async-done(((bf16[1,256,256]{2,1,0:T(8,128)(2,1)}), bf16[8,256,256]{2,1,0:T(8,128)(2,1)}) %all-gather.5.cloned.1.call-update) | async-done | bytes 1048592 | tf_op jit(solution)/shard_map/all_gather | solution.py:112
  94.1 270.2 %while.18 = (s32[]{:T(128)}, bf16[4,4,80,2048]{3,2,1,0:T(8,128)(2,1)}, bf16[4,4,80,256]{3,2,1,0:T(8,128)(2,1)}, bf16[4,4,80,256]{3,2,1,0:T(8,128)(2,1)}, f32[4,4...) while((s32[]{:T(128)}, ...), condition=%wide.region_4.6_spmd, body=%wide.region_0.5_spmd.sunk | while | flops 2675333632 | bytes 186917328 | solution.py:126
  98.5 2.6 gather_fusion.1
  101.1 2.6 gather_fusion
  103.8 2.4 broadcast_select_fusion.3
  115.5 3.6 fusion.126
  122.7 5.7 fusion.135
  129.5 4.4 fusion.128
  133.9 2.3 fusion.131
  136.2 2.4 fusion.129
  138.7 2.1 fusion.136
  140.8 2.6 copy.199
  143.4 2.3 fusion.134
  154.2 3.2 convert_element_type.153
  157.5 2.7 constant_dynamic-update-slice_fusion.8
  166.1 2.6 gather_fusion.1
  168.7 2.6 gather_fusion
  171.3 2.4 broadcast_select_fusion.3
  183.1 3.6 fusion.126
  190.3 5.7 fusion.135
  197.1 4.4 fusion.128
  201.5 2.3 fusion.131
  203.8 2.4 fusion.129
  208.3 2.6 copy.199
  210.9 2.3 fusion.134
  221.8 3.2 convert_element_type.153
  225.0 2.7 constant_dynamic-update-slice_fusion.8
  233.6 2.6 gather_fusion.1
  236.2 2.6 gather_fusion
  238.8 2.4 broadcast_select_fusion.3
  250.6 3.6 fusion.126
  257.8 5.7 fusion.135
  264.6 4.4 fusion.128
  269.0 2.3 fusion.131
  271.3 2.4 fusion.129
  275.9 2.6 copy.199
  278.5 2.3 fusion.134
  289.3 3.2 convert_element_type.153
  292.5 2.7 constant_dynamic-update-slice_fusion.8
  301.2 2.6 gather_fusion.1
  303.8 2.6 gather_fusion
  306.4 2.4 broadcast_select_fusion.3
  318.2 3.6 fusion.126
  325.4 5.7 fusion.135
  332.2 4.4 fusion.128
  336.6 2.3 fusion.131
  338.9 2.4 fusion.129
  343.4 2.6 copy.199
  346.0 2.3 fusion.134
  356.9 3.2 convert_element_type.153
  360.1 2.7 constant_dynamic-update-slice_fusion.8
  364.3 4.8 convolution_convert_fusion.1
  369.2 5.5 copy.72
  374.7 25.1 %all-reduce.7.cloned.1.call-done = (bf16[1280,32]{0,1:T(8,128)(2,1)}, bf16[1280,32]{0,1:T(8,128)(2,1)}) async-done(((bf16[1280,32]{0,1:T(8,128)(2,1)}, bf16[1280,32]{0,1:T(8,128)(2,1)}), (bf16[1280,32]{0,1:T(8,128)(2,1)}, bf16[1280,32]{0,1:T(8,128)(2,1)})) %all-reduce.7.cloned.1.call-update) | async-done | bytes 163856 | tf_op jit(solution)/shard_map/psum | solution.py:169
  399.7 2.2 fusion.60
  402.0 4.2 fusion.58
  406.3 3.8 convolution_convert_fusion.2
  411.3 5.5 copy.70
  416.8 3.8 convolution_convert_fusion.3
  421.8 54.6 %all-reduce.5.cloned.1.call-done = (bf16[1280,32]{0,1:T(8,128)(2,1)}, bf16[32,2048]{1,0:T(8,128)(2,1)}) async-done(((bf16[1280,32]{0,1:T(8,128)(2,1)}, bf16[32,2048]{1,0:T(8,128)(2,1)}), (bf16[1280,32]{0,1:T(8,128)(2,1)}, bf16[32,2048]{1,0:T(8,128)(2,1)})) %all-reduce.5.cloned.1.call-update) | async-done | bytes 213008 | tf_op jit(solution)/shard_map/psum | solution.py:180
  479.6 63.9 %reduce-scatter.5.cloned.1.call-done = bf16[1,256,256]{2,1,0:T(8,128)(2,1)} async-done(((bf16[8,256,256]{2,1,0:T(8,128)(2,1)}), bf16[1,256,256]{2,1,0:T(8,128)(2,1)}) %reduce-scatter.5.cloned.1.call-update) | async-done | bytes 131088 | tf_op jit(solution)/shard_map/reduce_scatter | solution.py:161
  543.4 66.7 %reduce-scatter.3.cloned.1.call-done = bf16[1,256,256]{2,1,0:T(8,128)(2,1)} async-done(((bf16[8,256,256]{2,1,0:T(8,128)(2,1)}), bf16[1,256,256]{2,1,0:T(8,128)(2,1)}) %reduce-scatter.3.cloned.1.call-update) | async-done | bytes 131088 | tf_op jit(solution)/shard_map/reduce_scatter | solution.py:158
  (280 shorter events, 128.5 us)
Async XLA Ops:
  7.2 3.1 copy-start
  7.2 45.8 %all-gather.3.cloned.1.call-start = ((), (), s32[]{:S(2)}) async-start(), calls=%async_computation.2 | async-start | bytes 1179648 | tf_op jit(solution)/shard_map/all_gather | solution.py:111
  7.9 86.2 %all-gather.5.cloned.1.call-start = ((), (), s32[]{:S(2)}) async-start(), calls=%async_computation.3 | async-start | bytes 1179648 | tf_op jit(solution)/shard_map/all_gather | solution.py:112
  8.7 391.1 %all-reduce.7.cloned.1.call-start = ((), (), s32[]{:S(2)}) async-start(), calls=%async_computation.7 | async-start | bytes 327680 | tf_op jit(solution)/shard_map/psum | solution.py:169
  111.8 7.3 %copy-start.3 = (bf16[40,8,16,128]{3,2,1,0:T(8,128)(2,1)}, bf16[40,8,16,128]{3,2,1,0:T(8,128)(2,1)S(1)}, u32[]{:S(2)}) copy-start(bf16[40,8,16,128]{3,2,1,0:T(8,128)(2,1)S(1)} %copy.196) | copy-start | bytes 3932164 | tf_op jit(solution)/shard_map/while
  114.1 5.0 copy-start.1
  115.4 3.8 copy-start.9
  122.7 5.7 copy-start.10
  122.7 5.7 copy-start.14
  122.7 6.5 %copy-start.4 = (bf16[40,8,16,128]{3,2,1,0:T(8,128)(2,1)S(1)}, bf16[40,8,16,128]{3,2,1,0:T(8,128)(2,1)}, u32[]{:S(2)}) copy-start(bf16[40,8,16,128]{3,2,1,0:T(8,128)(2,1)} %copy-done.3) | copy-start | bytes 3932164 | tf_op jit(solution)/shard_map/while
  128.5 5.4 slice-start
  129.5 4.4 slice-start.1
  136.2 2.5 copy-start.7
  136.2 2.5 copy-start.2
  148.1 3.8 copy-start.6
  148.1 3.8 copy-start.8
  157.4 2.7 copy-start.12
  157.4 2.7 copy-start.13
  179.4 7.3 %copy-start.3 = (bf16[40,8,16,128]{3,2,1,0:T(8,128)(2,1)}, bf16[40,8,16,128]{3,2,1,0:T(8,128)(2,1)S(1)}, u32[]{:S(2)}) copy-start(bf16[40,8,16,128]{3,2,1,0:T(8,128)(2,1)S(1)} %copy.196) | copy-start | bytes 3932164 | tf_op jit(solution)/shard_map/while
  181.7 5.0 copy-start.1
  182.9 3.8 copy-start.9
  190.3 5.7 copy-start.10
  190.3 5.7 copy-start.14
  190.3 6.5 %copy-start.4 = (bf16[40,8,16,128]{3,2,1,0:T(8,128)(2,1)S(1)}, bf16[40,8,16,128]{3,2,1,0:T(8,128)(2,1)}, u32[]{:S(2)}) copy-start(bf16[40,8,16,128]{3,2,1,0:T(8,128)(2,1)} %copy-done.3) | copy-start | bytes 3932164 | tf_op jit(solution)/shard_map/while
  196.0 5.4 slice-start
  197.1 4.4 slice-start.1
  203.8 2.5 copy-start.7
  203.8 2.5 copy-start.2
  215.7 3.8 copy-start.6
  215.7 3.8 copy-start.8
  225.0 2.7 copy-start.12
  225.0 2.7 copy-start.13
  246.9 7.3 %copy-start.3 = (bf16[40,8,16,128]{3,2,1,0:T(8,128)(2,1)}, bf16[40,8,16,128]{3,2,1,0:T(8,128)(2,1)S(1)}, u32[]{:S(2)}) copy-start(bf16[40,8,16,128]{3,2,1,0:T(8,128)(2,1)S(1)} %copy.196) | copy-start | bytes 3932164 | tf_op jit(solution)/shard_map/while
  249.2 5.0 copy-start.1
  250.4 3.8 copy-start.9
  257.8 5.7 copy-start.10
  257.8 5.7 copy-start.14
  257.8 6.5 %copy-start.4 = (bf16[40,8,16,128]{3,2,1,0:T(8,128)(2,1)S(1)}, bf16[40,8,16,128]{3,2,1,0:T(8,128)(2,1)}, u32[]{:S(2)}) copy-start(bf16[40,8,16,128]{3,2,1,0:T(8,128)(2,1)} %copy-done.3) | copy-start | bytes 3932164 | tf_op jit(solution)/shard_map/while
  263.6 5.4 slice-start
  264.6 4.4 slice-start.1
  271.3 2.5 copy-start.7
  271.3 2.5 copy-start.2
  283.2 3.8 copy-start.6
  283.2 3.8 copy-start.8
  292.5 2.7 copy-start.12
  292.5 2.7 copy-start.13
  314.5 7.3 %copy-start.3 = (bf16[40,8,16,128]{3,2,1,0:T(8,128)(2,1)}, bf16[40,8,16,128]{3,2,1,0:T(8,128)(2,1)S(1)}, u32[]{:S(2)}) copy-start(bf16[40,8,16,128]{3,2,1,0:T(8,128)(2,1)S(1)} %copy.196) | copy-start | bytes 3932164 | tf_op jit(solution)/shard_map/while
  316.8 5.0 copy-start.1
  318.0 3.8 copy-start.9
  325.4 5.7 copy-start.10
  325.4 5.7 copy-start.14
  325.4 6.5 %copy-start.4 = (bf16[40,8,16,128]{3,2,1,0:T(8,128)(2,1)S(1)}, bf16[40,8,16,128]{3,2,1,0:T(8,128)(2,1)}, u32[]{:S(2)}) copy-start(bf16[40,8,16,128]{3,2,1,0:T(8,128)(2,1)} %copy-done.3) | copy-start | bytes 3932164 | tf_op jit(solution)/shard_map/while
  331.1 5.4 slice-start
  332.2 4.4 slice-start.1
  338.9 2.5 copy-start.7
  338.9 2.5 copy-start.2
  350.8 3.8 copy-start.6
  350.8 3.8 copy-start.8
  360.1 2.7 copy-start.12
  360.1 2.7 copy-start.13
  369.1 107.2 %all-reduce.5.cloned.1.call-start = ((), (), s32[]{:S(2)}) async-start(), calls=%async_computation.6 | async-start | bytes 425984 | tf_op jit(solution)/shard_map/psum | solution.py:180
  402.0 4.3 copy-start.16
  406.2 137.2 %reduce-scatter.5.cloned.1.call-start = ((), (), s32[]{:S(2)}) async-start(), calls=%async_computation.5 | async-start | bytes 1179648 | tf_op jit(solution)/shard_map/reduce_scatter | solution.py:161
  411.3 198.9 %reduce-scatter.3.cloned.1.call-start = ((), (), s32[]{:S(2)}) async-start(), calls=%async_computation.4 | async-start | bytes 1179648 | tf_op jit(solution)/shard_map/reduce_scatter | solution.py:158
  (9 other events, 12.0 us)
Sparse Core Ops, SparseCore 0:
  10.1 42.8 all-gather.2
  55.1 38.8 all-gather.4
  369.3 30.4 all-reduce.6
  406.3 70.0 all-reduce.4
  480.2 63.1 reduce-scatter.4
  547.6 62.4 reduce-scatter.2
where the time goes:
time: 620 us; the launch traced here: 617 us
  waiting for transfers between devices  293 us (47%)
  local copies, waits for them, and re-layouts  159 us (26%)
  matrix products  136 us (22%)
  between operations  14.2 us (2%)
  other arithmetic  13.6 us (2%)
    reduce_scatter x1, waiting for transfers between devices, shards(): lax.psum_scatter(key_buffer.astype(jnp.bfloat16), 'dp', scatter_dimension...  66.7 us
    reduce_scatter x1, waiting for transfers between devices, shards(): lax.psum_scatter(value_buffer.astype(jnp.bfloat16), 'dp', scatter_dimensi...  63.9 us
    psum x1, waiting for transfers between devices, shards(): lax.psum(down_term.astype(jnp.bfloat16), 'dp').astype(jnp.float32)  54.6 us
    all_gather x1, waiting for transfers between devices, shards(): lax.all_gather(prompt_token_values, 'dp', axis=0, tiled=True)  41.1 us
    all_gather x1, waiting for transfers between devices, shards(): lax.all_gather(prompt_token_keys, 'dp', axis=0, tiled=True)  40.2 us
    psum x1, waiting for transfers between devices, shards(): back_sum = lax.psum(backward_piece.astype(jnp.bfloat16), 'mp')  25.1 us
    dynamic_update_slice x12, local copies, waits for them, and re-layouts, shards(): lax.map(one_block, (batched(queries), batched(response_keys), batched(res...  24.3 us
    dynamic_slice x16, local copies, waits for them, and re-layouts, shards(): lax.map(one_block, (batched(queries), batched(response_keys), batched(res...  23.6 us
  transfers between devices with their start and end apart: 6, of which 6 were waited for; matrix products, arithmetic and copies ran while one was open for 5% of the time, Pallas kernels for 0%

commit v1 on v0

v1 whole, which is shorter than its diff:
```python
import functools
import math

import jax
import jax.numpy as jnp
import numpy as np
from jax import lax
from jax.experimental import pallas as pl
from jax.experimental.pallas import tpu as pltpu
from jax.sharding import PartitionSpec as P

QUERY_HEAD_COUNT = 64
KEY_VALUE_HEADS = 8
HEAD_SIZE = 128
QUERY_GROUP = QUERY_HEAD_COUNT // KEY_VALUE_HEADS
ROW_STEP = 16
CUTS = 2

adapter_scale = 2.0
MESH = pl.DeviceIdType.MESH
F32 = jnp.float32
BF16 = jnp.bfloat16
NT = (((1,), (1,)), ((), ()))


def ring_place(index, n):
    odd = index % 2
    return (1 - odd) * (index // 2) + odd * (n - 1 - index // 2)


def ring_member(place, n):
    place = (place + 2 * n) % n
    upper = place // (n // 2)
    return (1 - upper) * (2 * place) + upper * (2 * (n - 1 - place) + 1)


def enter(dp_peers, mp_peers):
    barrier = pltpu.get_barrier_semaphore()
    for peer in dp_peers:
        pl.semaphore_signal(barrier, inc=1, device_id={"dp": peer}, device_id_type=MESH)
    for peer in mp_peers:
        pl.semaphore_signal(barrier, inc=1, device_id={"mp": peer}, device_id_type=MESH)
    pl.semaphore_wait(barrier, len(dp_peers) + len(mp_peers))


def remote(source, target, send, recv, peer):
    return pltpu.make_async_remote_copy(
        src_ref=source, dst_ref=target, send_sem=send, recv_sem=recv,
        device_id=peer, device_id_type=MESH,
    )


def gather_kernel(
    n, m, pk, pv, hidden, down, gk, gv, inner,
    pieces, ksend, krecv, vsend, vrecv, msend, mrecv,
):
    me = lax.axis_index("dp")
    mine = lax.axis_index("mp")
    place = ring_place(me, n)
    right, left = ring_member(place + 1, n), ring_member(place + n - 1, n)
    mp_peers = [lax.rem(mine + d, m) for d in range(1, m)]
    enter([right, left], mp_peers)

    rows = pk.shape[0] // CUTS
    tokens = hidden.shape[0]
    piece_count = max(1, min(5, tokens // 256))
    piece = tokens // piece_count
    down_rows = down[...]
    kcopies, vcopies, mcopies = [], [], []

    def inner_piece(j):
        span = pl.ds(j * piece, piece)
        pieces[mine, :, span] = lax.dot_general(
            down_rows, hidden[span, :], NT, preferred_element_type=F32
        ).astype(BF16)

    def exchange():
        for d, peer in enumerate(mp_peers):
            copy = remote(
                pieces.at[mine], pieces.at[mine], msend.at[d], mrecv.at[d], {"mp": peer}
            )
            copy.start()
            mcopies.append(copy)

    done = 0
    for step in range(n - 1):
        kowner = ring_member(place + n - step, n)
        vowner = ring_member(place + step, n)
        krow, vrow = [], []
        for cut in range(CUTS):
            span = pl.ds(cut * rows, rows)
            for owner, own, whole, send, recv, to, row, before in (
                (kowner, pk, gk, ksend, krecv, right, krow, kcopies),
                (vowner, pv, gv, vsend, vrecv, left, vrow, vcopies),
            ):
                if step:
                    before[-1][cut].wait_recv()
                copy = remote(
                    own.at[span] if step == 0 else whole.at[owner, span],
                    whole.at[owner, span],
                    send.at[step, cut], recv.at[step, cut], {"dp": to},
                )
                copy.start()
                row.append(copy)
        kcopies.append(krow)
        vcopies.append(vrow)
        if step == 0:
            gk[me] = pk[...]
            gv[me] = pv[...]
        if done < piece_count:
            inner_piece(done)
            done += 1
            if done == piece_count:
                exchange()
    for copy in kcopies[-1] + vcopies[-1]:
        copy.wait_recv()
    for copy in mcopies:
        copy.wait_recv()
    total = pieces[0].astype(F32)
    for j in range(1, m):
        total = total + pieces[j].astype(F32)
    inner[...] = total.astype(BF16)
    for row in kcopies + vcopies + [mcopies]:
        for copy in row:
            copy.wait_send()


def gather(n, m, pk, pv, hidden, down_rows):
    rank = down_rows.shape[0]
    tokens = hidden.shape[0]
    vmem = pl.BlockSpec(memory_space=pltpu.VMEM)
    return pl.pallas_call(
        functools.partial(gather_kernel, n, m),
        out_shape=(
            jax.ShapeDtypeStruct((n,) + pk.shape, BF16),
            jax.ShapeDtypeStruct((n,) + pv.shape, BF16),
            jax.ShapeDtypeStruct((rank, tokens), BF16),
        ),
        in_specs=[vmem] * 4,
        out_specs=(vmem,) * 3,
        scratch_shapes=[
            pltpu.VMEM((m, rank, tokens), BF16),
            pltpu.SemaphoreType.DMA((n - 1, CUTS)),
            pltpu.SemaphoreType.DMA((n - 1, CUTS)),
            pltpu.SemaphoreType.DMA((n - 1, CUTS)),
            pltpu.SemaphoreType.DMA((n - 1, CUTS)),
            pltpu.SemaphoreType.DMA((m - 1,)),
            pltpu.SemaphoreType.DMA((m - 1,)),
        ],
        compiler_params=pltpu.CompilerParams(
            collective_id=0, has_side_effects=True, vmem_limit_bytes=56 * 2**20
        ),
        name="gather_prompts",
    )(pk, pv, hidden, down_rows)


def attention_kernel(
    owners, lengths, q, g, ko, vo, gk, gv, places,
    dq, dko, dvo, kb, vb, kacc, vacc,
):
    r = pl.program_id(0)
    prompt = owners[r]
    length = lengths[r]
    slots = q.shape[1]
    prompt_rows = gk.shape[1]
    kv_heads = gk.shape[2] // HEAD_SIZE
    score_scale = 1.0 / math.sqrt(HEAD_SIZE)

    @pl.when(r == 0)
    def _():
        kacc[...] = jnp.zeros_like(kacc)
        vacc[...] = jnp.zeros_like(vacc)

    def part(count):
        alive = (lax.broadcasted_iota(jnp.int32, (count, HEAD_SIZE), 0) < length)
        alive = alive.astype(F32).astype(BF16)
        width = QUERY_GROUP * count
        place = places[count // ROW_STEP - 1, 0:1, 0:width]
        own_row = lax.broadcasted_iota(jnp.int32, (count, width), 0)
        visible = (own_row <= place) & (own_row < length)
        if count < slots:
            dq[0, count:, :] = jnp.zeros((slots - count, dq.shape[2]), BF16)
            dko[0, count:, :] = jnp.zeros((slots - count, dko.shape[2]), BF16)
            dvo[0, count:, :] = jnp.zeros((slots - count, dvo.shape[2]), BF16)
        for head in range(kv_heads):
            lanes = slice(head * HEAD_SIZE, (head + 1) * HEAD_SIZE)
            first = head * QUERY_GROUP

            def columns(h):
                return slice((first + h) * HEAD_SIZE, (first + h + 1) * HEAD_SIZE)

            queries = jnp.concatenate(
                [q[0, :count, columns(h)] for h in range(QUERY_GROUP)], axis=0
            )
            grads = jnp.concatenate(
                [g[0, :count, columns(h)] * alive for h in range(QUERY_GROUP)], axis=0
            )
            keys = jnp.concatenate([gk[prompt, :, lanes], ko[0, :count, lanes]], axis=0)
            values = jnp.concatenate([gv[prompt, :, lanes], vo[0, :count, lanes]], axis=0)
            scores = lax.dot_general(keys, queries, NT, preferred_element_type=F32)
            powers = jnp.exp2(scores * (score_scale * math.log2(math.e)))
            powers = jnp.concatenate(
                [powers[:prompt_rows], jnp.where(visible, powers[prompt_rows:], 0.0)], axis=0
            )
            inverse = 1.0 / jnp.sum(powers, axis=0, keepdims=True)
            weight_grad = lax.dot_general(values, grads, NT, preferred_element_type=F32)
            weights = powers * inverse
            row_dot = jnp.sum(weights * weight_grad, axis=0, keepdims=True)
            low = weights.astype(BF16)
            score_grad = (weights * (weight_grad - row_dot)).astype(BF16)
            turned = jnp.dot(keys.T, score_grad, preferred_element_type=F32) * score_scale
            query_part = turned.T.astype(BF16)
            for h in range(QUERY_GROUP):
                dq[0, :count, columns(h)] = query_part[h * count : (h + 1) * count]
            key_part = jnp.dot(score_grad, queries, preferred_element_type=F32) * score_scale
            value_part = jnp.dot(low, grads, preferred_element_type=F32)
            kacc[prompt, :, lanes] += key_part[:prompt_rows]
            vacc[prompt, :, lanes] += value_part[:prompt_rows]
            dko[0, :count, lanes] = key_part[prompt_rows:].astype(BF16)
            dvo[0, :count, lanes] = value_part[prompt_rows:].astype(BF16)

    steps = slots // ROW_STEP
    level = (length + (ROW_STEP - 1)) // ROW_STEP
    for k in range(1, steps + 1):
        pl.when(level == k)(functools.partial(part, k * ROW_STEP))

    @pl.when(r == pl.num_programs(0) - 1)
    def _():
        kb[...] = kacc[...].astype(BF16)
        vb[...] = vacc[...].astype(BF16)


def attention(owners, lengths, q, g, ko, vo, gk, gv):
    count, slots, width = q.shape
    own_width = ko.shape[2]
    steps = slots // ROW_STEP
    table = np.zeros((steps, 8, QUERY_GROUP * slots), np.int32)
    for k in range(1, steps + 1):
        used = QUERY_GROUP * k * ROW_STEP
        table[k - 1, :, :used] = np.arange(used, dtype=np.int32) % (k * ROW_STEP)

    def each(last):
        return pl.BlockSpec((1, slots, last), lambda r, *_: (r, 0, 0))

    def whole(shape):
        return pl.BlockSpec(
            shape, lambda r, *_: (0,) * len(shape), pipeline_mode=pl.Buffered(1)
        )

    def whole_out(shape):
        return pl.BlockSpec(shape, lambda r, *_: (0,) * len(shape))

    return pl.pallas_call(
        attention_kernel,
        grid_spec=pltpu.PrefetchScalarGridSpec(
            num_scalar_prefetch=2,
            grid=(count,),
            in_specs=[
                each(width), each(width), each(own_width), each(own_width),
                whole(gk.shape), whole(gv.shape), whole(table.shape),
            ],
            out_specs=[
                each(width), each(own_width), each(own_width),
                whole_out(gk.shape), whole_out(gv.shape),
            ],
            scratch_shapes=[pltpu.VMEM(gk.shape, F32), pltpu.VMEM(gv.shape, F32)],
        ),
        out_shape=(
            jax.ShapeDtypeStruct(q.shape, BF16),
            jax.ShapeDtypeStruct(ko.shape, BF16),
            jax.ShapeDtypeStruct(vo.shape, BF16),
            jax.ShapeDtypeStruct(gk.shape, BF16),
            jax.ShapeDtypeStruct(gv.shape, BF16),
        ),
        compiler_params=pltpu.CompilerParams(vmem_limit_bytes=60 * 2**20),
        name="attention_backward",
    )(owners, lengths, q, g, ko, vo, gk, gv, jnp.asarray(table))


def reduce_kernel(
    n, m, product, kb, vb, inner, up, hidden_far, dq_far,
    pk_out, pv_out, down_out, up_out,
    hidden, dq, kslots, vslots, pieces, terms, shares, final,
    ksend, krecv, vsend, vrecv, msend, mrecv, rsend, rrecv, fsend, frecv, lsem,
):
    me = lax.axis_index("dp")
    mine = lax.axis_index("mp")
    place = ring_place(me, n)
    right, left = ring_member(place + 1, n), ring_member(place + n - 1, n)
    dp_peers = [lax.rem(me + d, n) for d in range(1, n)]
    mp_peers = [lax.rem(mine + d, m) for d in range(1, m)]
    dq_copy = pltpu.make_async_copy(dq_far, dq, lsem.at[0])
    dq_copy.start()
    hidden_copy = pltpu.make_async_copy(hidden_far, hidden, lsem.at[1])
    hidden_copy.start()
    enter(dp_peers, mp_peers)

    rows = kb.shape[1] // CUTS
    lane_blocks = terms.shape[2] // 128
    down_blocks = hidden.shape[1] // 128
    up_blocks = dq.shape[1] // 128
    kcopies, vcopies, mcopies, rcopies, fcopies = [], [], [], [], []

    def ring(step):
        krow, vrow = [], []
        for cut in range(CUTS):
            span = pl.ds(cut * rows, rows)
            for owner, own, slot, send, recv, to, row, before in (
                (ring_member(place + n - 1 - step, n), kb, kslots, ksend, krecv, right, krow, kcopies),
                (ring_member(place + 1 + step, n), vb, vslots, vsend, vrecv, left, vrow, vcopies),
            ):
                if step:
                    before[-1][cut].wait_recv()
                    slot[step - 1, span] = (
                        slot[step - 1, span].astype(F32) + own[owner, span].astype(F32)
                    ).astype(BF16)
                copy = remote(
                    own.at[owner, span] if step == 0 else slot.at[step - 1, span],
                    slot.at[step, span],
                    send.at[step, cut], recv.at[step, cut], {"dp": to},
                )
                copy.start()
                row.append(copy)
        kcopies.append(krow)
        vcopies.append(vrow)

    def back():
        dq_copy.wait()
        pieces[mine] = lax.dot_general(
            up[...], dq[...], NT, preferred_element_type=F32
        ).astype(BF16)
        for d, peer in enumerate(mp_peers):
            copy = remote(
                pieces.at[mine], pieces.at[mine], msend.at[d], mrecv.at[d], {"mp": peer}
            )
            copy.start()
            mcopies.append(copy)

    def put(block, values):
        at = block % lane_blocks * 128
        terms[block // lane_blocks, :, at : at + 128] = values

    def up_term():
        term = jnp.dot(inner[...], dq[...], preferred_element_type=F32) * product
        term = term.astype(BF16)
        for b in range(up_blocks):
            put(down_blocks + b, term[:, b * 128 : (b + 1) * 128])
        for b in range(down_blocks + up_blocks, n * lane_blocks):
            put(b, jnp.zeros((terms.shape[1], 128), BF16))

    def down_term():
        hidden_copy.wait()
        for copy in mcopies:
            copy.wait_recv()
        total = pieces[0].astype(F32)
        for j in range(1, m):
            total = total + pieces[j].astype(F32)
        term = jnp.dot(total.astype(BF16), hidden[...], preferred_element_type=F32) * product
        term = term.astype(BF16)
        for b in range(down_blocks):
            put(b, term[:, b * 128 : (b + 1) * 128])
        for d, peer in enumerate(dp_peers):
            copy = remote(
                terms.at[peer], shares.at[me], rsend.at[d], rrecv.at[d], {"dp": peer}
            )
            copy.start()
            rcopies.append(copy)
        shares[me] = terms[me]

    def sum_terms():
        for copy in rcopies:
            copy.wait_recv()
        total = shares[0].astype(F32)
        for j in range(1, n):
            total = total + shares[j].astype(F32)
        final[me] = total.astype(BF16)
        for d, peer in enumerate(dp_peers):
            copy = remote(
                final.at[me], final.at[me], fsend.at[d], frecv.at[d], {"dp": peer}
            )
            copy.start()
            fcopies.append(copy)

    todo = {0: [back], 1: [up_term], 2: [down_term], 4: [sum_terms]}
    for step in range(n - 1):
        ring(step)
        for action in todo.get(step, ()):
            action()
    for cut in range(CUTS):
        span = pl.ds(cut * rows, rows)
        for own, slot, out, last in (
            (kb, kslots, pk_out, kcopies[-1]), (vb, vslots, pv_out, vcopies[-1]),
        ):
            last[cut].wait_recv()
            out[span] = (
                slot[n - 2, span].astype(F32) + own[me, span].astype(F32)
            ).astype(BF16)
    for copy in fcopies:
        copy.wait_recv()
    for b in range(down_blocks + up_blocks):
        at = b % lane_blocks * 128
        block = final[b // lane_blocks, :, at : at + 128].astype(F32)
        if b < down_blocks:
            down_out[:, b * 128 : (b + 1) * 128] = block
        else:
            up_out[:, (b - down_blocks) * 128 : (b - down_blocks + 1) * 128] = block
    for row in kcopies + vcopies + [mcopies, rcopies, fcopies]:
        for copy in row:
            copy.wait_send()


def reduce(n, m, product, kb, vb, inner, up, hidden, dq):
    rank = up.shape[0]
    tokens, depth = hidden.shape
    width = dq.shape[1]
    lanes = -(-(depth + width) // (128 * n)) * 128
    vmem = pl.BlockSpec(memory_space=pltpu.VMEM)
    far = pl.BlockSpec(memory_space=pl.ANY)
    block = kb.shape[1:]
    dma = pltpu.SemaphoreType.DMA
    return pl.pallas_call(
        functools.partial(reduce_kernel, n, m, product),
        out_shape=(
            jax.ShapeDtypeStruct(block, BF16),
            jax.ShapeDtypeStruct(block, BF16),
            jax.ShapeDtypeStruct((rank, depth), F32),
            jax.ShapeDtypeStruct((rank, width), F32),
        ),
        in_specs=[vmem] * 4 + [far] * 2,
        out_specs=(vmem,) * 4,
        scratch_shapes=[
            pltpu.VMEM((tokens, depth), BF16),
            pltpu.VMEM((tokens, width), BF16),
            pltpu.VMEM((n - 1,) + block, BF16),
            pltpu.VMEM((n - 1,) + block, BF16),
            pltpu.VMEM((m, rank, tokens), BF16),
            pltpu.VMEM((n, rank, lanes), BF16),
            pltpu.VMEM((n, rank, lanes), BF16),
            pltpu.VMEM((n, rank, lanes), BF16),
            dma((n - 1, CUTS)), dma((n - 1, CUTS)), dma((n - 1, CUTS)), dma((n - 1, CUTS)),
            dma((m - 1,)), dma((m - 1,)),
            dma((n - 1,)), dma((n - 1,)), dma((n - 1,)), dma((n - 1,)),
            dma((2,)),
        ],
        compiler_params=pltpu.CompilerParams(
            collective_id=1, has_side_effects=True, vmem_limit_bytes=56 * 2**20
        ),
        name="reduce_gradients",
    )(kb, vb, inner, up, hidden, dq)


def shards(
    queries,
    response_keys,
    response_values,
    output_gradient,
    prompt_token_keys,
    prompt_token_values,
    normed_hidden_input,
    adapter_down_factor,
    adapter_up_factor,
    response_prompt_index,
    response_lengths,
):
    n, m = lax.axis_size("dp"), lax.axis_size("mp")
    hidden = normed_hidden_input.reshape(-1, normed_hidden_input.shape[2])
    gk, gv, inner = gather(
        n, m, prompt_token_keys[0], prompt_token_values[0], hidden, adapter_down_factor.T
    )
    dq, dko, dvo, kb, vb = attention(
        response_prompt_index, response_lengths, queries, output_gradient,
        response_keys, response_values, gk, gv,
    )
    product = adapter_scale / math.sqrt(hidden.shape[0] * n)
    pk, pv, down, up = reduce(
        n, m, product, kb, vb, inner, adapter_up_factor, hidden,
        dq.reshape(-1, dq.shape[2]),
    )
    return dq, dko, dvo, pk[None], pv[None], down.T, up


def solution(mesh):
    rows = P("dp", None, "mp")
    placed = (rows,) * 7 + (P("mp", None), P(None, "mp"), P("dp"), P("dp"))
    return jax.shard_map(
        shards,
        mesh=mesh,
        in_specs=placed,
        out_specs=(rows,) * 5 + (P("mp", None), P(None, "mp")),
        check_vma=False,
    )
```

time: 620 us -> 114 us (0.18)
  waiting for transfers between devices: 293 us -> 0 us
  local copies, waits for them, and re-layouts: 159 us -> 6.4 us
  matrix products: 136 us -> 0 us
  Pallas kernels: 0 us -> 107 us
  other arithmetic: 13.6 us -> 0 us
  between operations: 14.2 us -> 0.66 us
    dot_general x54 -> x0, matrix products: 136 us -> none  [the longest x4 22.9 us: respond(): jnp.einsum('gclm,lgcd->mgd', front_low, grad_live, preferred_element_type...]
    reduce_scatter x2 -> x0, waiting for transfers between devices: 131 us -> none  [the longest x1 66.7 us: shards(): lax.psum_scatter(key_buffer.astype(jnp.bfloat16), 'dp', scatter_dimension...]
    pallas_call x0 -> x3, Pallas kernels: none -> 107 us  [the longest x1 41.4 us: reduce(): pl.pallas_call(functools.partial(reduce_kernel, n, m, product), out_shape...]
    all_gather x2 -> x0, waiting for transfers between devices: 81.3 us -> none  [the longest x1 41.1 us: shards(): lax.all_gather(prompt_token_values, 'dp', axis=0, tiled=True)]
    psum x2 -> x0, waiting for transfers between devices: 79.7 us -> none  [the longest x1 54.6 us: shards(): lax.psum(down_term.astype(jnp.bfloat16), 'dp').astype(jnp.float32)]
    convert_element_type x30 -> x0, local copies, waits for them, and re-layouts: 51.3 us -> none  [the longest x8 18.7 us: respond(): query_part.reshape(row_count, -1).astype(jnp.bfloat16)]
    reshape x20 -> x0, local copies, waits for them, and re-layouts: 34.9 us -> none  [the longest x2 10.9 us: shards(): array.reshape((GROUP,) + array.shape[2:])]
    dynamic_update_slice x12 -> x0, local copies, waits for them, and re-layouts: 24.3 us -> none  [shards(): lax.map(one_block, (batched(queries), batched(response_keys), batched(res...]
  transfers between devices with their start and end apart: 6 -> 0, of which waited for: 6 -> 0; matrix products, arithmetic and copies ran while one was open for 5% -> 0% of each run, Pallas kernels for 0% -> 0%
where the time goes in v1:
time: 114 us
  Pallas kernels  107 us (94%)
  local copies, waits for them, and re-layouts  6.4 us (6%)
    pallas_call x1, Pallas kernels, reduce(): pl.pallas_call(functools.partial(reduce_kernel, n, m, product), out_shape...  41.4 us
    pallas_call x1, Pallas kernels, gather(): pl.pallas_call(functools.partial(gather_kernel, n, m), out_shape=(jax.Sha...  35.6 us
    pallas_call x1, Pallas kernels, attention(): pl.pallas_call(attention_kernel, grid_spec=pltpu.PrefetchScalarGridSpec(n...  29.7 us
    unnamed x4, local copies, waits for them, and re-layouts  6.4 us

profile of v1, /device:TPU:0, one launch (start us, length us, event | category | flops | bytes accessed | tf_op | source)
XLA Modules:
  0.0 113.8 jit_solution(17807417448819473656)
XLA Ops:
  0.6 35.6 %gather_prompts.1 = (bf16[8,256,256]{2,1,0:T(8,128)(2,1)}, bf16[8,256,256]{2,1,0:T(8,128)(2,1)}, bf16[32,1280]{1,0:T(8,128)(2,1)}) custom-call(bf16[256,256]{1,0:T(8,128)(2,1)} %bitcast.12, bf16[256,256]{1,0:T(8,128)(2,1)} %bitcast.13, bf16[1280,1280]{1,0:T(8,128)(2,1)} %bitcast.8, bf16[32,1280]{1,0:T(8,128)(2,1)} %bitcast.16), custom_call_target="tpu_custom_call" | custom-call | tf_op jit(solution)/shard_map/gather_prompts/pallas_call | solution.py:132
  36.2 29.7 %attention_backward.1 = (bf16[16,80,2048]{2,1,0:T(8,128)(2,1)}, bf16[16,80,256]{2,1,0:T(8,128)(2,1)}, bf16[16,80,256]{2,1,0:T(8,128)(2,1)}, bf16[8,256,256]{2,1,0:T(8,128)(2,1)}, bf16[8,256,256]{2,1,0:T(8,128)(2,1)}) custom-call(s32[16]{0:T(128)} %owners.1, s32[16]{0:T(128)} %lengths.1, bf16[16,80,2048]{2,1,0:T(8,128)(2,1)} %q.1, bf16[16,80,2048]{2,1,0:T(8,128)(2,1)} %g.1, ...), custom_call_target="tpu_custom_call" | custom-call | tf_op jit(solution)/shard_map/attention_backward/pallas_call | solution.py:253
  65.9 41.4 %reduce_gradients.1 = (bf16[256,256]{1,0:T(8,128)(2,1)}, bf16[256,256]{1,0:T(8,128)(2,1)}, f32[32,1280]{1,0:T(8,128)}, f32[32,2048]{1,0:T(8,128)}) custom-call(bf16[8,256,256]{2,1,0:T(8,128)(2,1)} %get-tuple-element.24.kb, bf16[8,256,256]{2,1,0:T(8,128)(2,1)} %get-tuple-element.25.vb, bf16[32,1280]{1,0:T(8,128)(2,1)} %get-tuple-element.26.inner, ...), custom_call_target="tpu_custom_call" | custom-call | tf_op jit(solution)/shard_map/reduce_gradients/pallas_call | solution.py:421
  107.4 1.6 %copy.23 = bf16[1,256,256]{2,1,0:T(8,128)(2,1)} copy(bf16[1,256,256]{2,1,0:T(8,128)(2,1)} %bitcast.15) | data formatting | bytes 262144
  108.9 1.6 %copy.24 = bf16[1,256,256]{2,1,0:T(8,128)(2,1)} copy(bf16[1,256,256]{2,1,0:T(8,128)(2,1)} %bitcast.14) | data formatting | bytes 262144
  110.5 1.6 %copy.25 = f32[1280,32]{0,1:T(8,128)} copy(f32[1280,32]{0,1:T(8,128)} %bitcast.11) | data formatting | bytes 327680
  112.1 1.7 %copy.26 = f32[32,2048]{1,0:T(8,128)} copy(f32[32,2048]{1,0:T(8,128)} %get-tuple-element.44) | data formatting | bytes 524288

commit v2 on v1

--- a/solution.py
+++ b/solution.py
@@ -51,14 +51,16 @@
 
 
 def gather_kernel(
-    n, m, pk, pv, hidden, down, gk, gv, inner,
-    pieces, ksend, krecv, vsend, vrecv, msend, mrecv,
+    n, m, pk, pv, hidden_far, down, gk, gv, inner,
+    hidden, pieces, ksend, krecv, vsend, vrecv, msend, mrecv, lsem,
 ):
     me = lax.axis_index("dp")
     mine = lax.axis_index("mp")
     place = ring_place(me, n)
     right, left = ring_member(place + 1, n), ring_member(place + n - 1, n)
     mp_peers = [lax.rem(mine + d, m) for d in range(1, m)]
+    hidden_copy = pltpu.make_async_copy(hidden_far, hidden, lsem.at[0])
+    hidden_copy.start()
     enter([right, left], mp_peers)
 
     rows = pk.shape[0] // CUTS
@@ -107,19 +109,20 @@
         if step == 0:
             gk[me] = pk[...]
             gv[me] = pv[...]
+            hidden_copy.wait()
         if done < piece_count:
             inner_piece(done)
             done += 1
             if done == piece_count:
                 exchange()
-    for copy in kcopies[-1] + vcopies[-1]:
-        copy.wait_recv()
     for copy in mcopies:
         copy.wait_recv()
     total = pieces[0].astype(F32)
     for j in range(1, m):
         total = total + pieces[j].astype(F32)
     inner[...] = total.astype(BF16)
+    for copy in kcopies[-1] + vcopies[-1]:
+        copy.wait_recv()
     for row in kcopies + vcopies + [mcopies]:
         for copy in row:
             copy.wait_send()
@@ -136,9 +139,10 @@
             jax.ShapeDtypeStruct((n,) + pv.shape, BF16),
             jax.ShapeDtypeStruct((rank, tokens), BF16),
         ),
-        in_specs=[vmem] * 4,
+        in_specs=[vmem, vmem, pl.BlockSpec(memory_space=pl.ANY), vmem],
         out_specs=(vmem,) * 3,
         scratch_shapes=[
+            pltpu.VMEM(hidden.shape, BF16),
             pltpu.VMEM((m, rank, tokens), BF16),
             pltpu.SemaphoreType.DMA((n - 1, CUTS)),
             pltpu.SemaphoreType.DMA((n - 1, CUTS)),
@@ -146,6 +150,7 @@
             pltpu.SemaphoreType.DMA((n - 1, CUTS)),
             pltpu.SemaphoreType.DMA((m - 1,)),
             pltpu.SemaphoreType.DMA((m - 1,)),
+            pltpu.SemaphoreType.DMA((1,)),
         ],
         compiler_params=pltpu.CompilerParams(
             collective_id=0, has_side_effects=True, vmem_limit_bytes=56 * 2**20
@@ -279,8 +284,8 @@
 
 def reduce_kernel(
     n, m, product, kb, vb, inner, up, hidden_far, dq_far,
-    pk_out, pv_out, down_out, up_out,
-    hidden, dq, kslots, vslots, pieces, terms, shares, final,
+    pk_out, pv_out, final,
+    hidden, dq, kslots, vslots, pieces, terms, shares,
     ksend, krecv, vsend, vrecv, msend, mrecv, rsend, rrecv, fsend, frecv, lsem,
 ):
     me = lax.axis_index("dp")
@@ -299,36 +304,42 @@
     lane_blocks = terms.shape[2] // 128
     down_blocks = hidden.shape[1] // 128
     up_blocks = dq.shape[1] // 128
+    tokens = hidden.shape[0]
+    piece_count = max(1, min(5, tokens // 256))
+    piece = tokens // piece_count
     kcopies, vcopies, mcopies, rcopies, fcopies = [], [], [], [], []
 
-    def ring(step):
-        krow, vrow = [], []
-        for cut in range(CUTS):
-            span = pl.ds(cut * rows, rows)
-            for owner, own, slot, send, recv, to, row, before in (
-                (ring_member(place + n - 1 - step, n), kb, kslots, ksend, krecv, right, krow, kcopies),
-                (ring_member(place + 1 + step, n), vb, vslots, vsend, vrecv, left, vrow, vcopies),
-            ):
-                if step:
-                    before[-1][cut].wait_recv()
-                    slot[step - 1, span] = (
-                        slot[step - 1, span].astype(F32) + own[owner, span].astype(F32)
-                    ).astype(BF16)
-                copy = remote(
-                    own.at[owner, span] if step == 0 else slot.at[step - 1, span],
-                    slot.at[step, span],
-                    send.at[step, cut], recv.at[step, cut], {"dp": to},
-                )
-                copy.start()
-                row.append(copy)
-        kcopies.append(krow)
-        vcopies.append(vrow)
-
-    def back():
-        dq_copy.wait()
-        pieces[mine] = lax.dot_general(
-            up[...], dq[...], NT, preferred_element_type=F32
+    def ring(step, cut):
+        if cut == 0:
+            kcopies.append([])
+            vcopies.append([])
+        span = pl.ds(cut * rows, rows)
+        for owner, own, slot, send, recv, to, copies in (
+            (ring_member(place + n - 1 - step, n), kb, kslots, ksend, krecv, right, kcopies),
+            (ring_member(place + 1 + step, n), vb, vslots, vsend, vrecv, left, vcopies),
+        ):
+            if step:
+                copies[step - 1][cut].wait_recv()
+                slot[step - 1, span] = (
+                    slot[step - 1, span].astype(F32) + own[owner, span].astype(F32)
+                ).astype(BF16)
+            copy = remote(
+                own.at[owner, span] if step == 0 else slot.at[step - 1, span],
+                slot.at[step, span],
+                send.at[step, cut], recv.at[step, cut], {"dp": to},
+            )
+            copy.start()
+            copies[step].append(copy)
+
+    def back(j):
+        if j == 0:
+            dq_copy.wait()
+        span = pl.ds(j * piece, piece)
+        pieces[mine, :, span] = lax.dot_general(
+            up[...], dq[span, :], NT, preferred_element_type=F32
         ).astype(BF16)
+
+    def send_back():
         for d, peer in enumerate(mp_peers):
             copy = remote(
                 pieces.at[mine], pieces.at[mine], msend.at[d], mrecv.at[d], {"mp": peer}
@@ -340,25 +351,34 @@
         at = block % lane_blocks * 128
         terms[block // lane_blocks, :, at : at + 128] = values
 
-    def up_term():
-        term = jnp.dot(inner[...], dq[...], preferred_element_type=F32) * product
+    def up_term(j):
+        at = j * 256
+        term = jnp.dot(inner[...], dq[:, at : at + 256], preferred_element_type=F32) * product
         term = term.astype(BF16)
-        for b in range(up_blocks):
-            put(down_blocks + b, term[:, b * 128 : (b + 1) * 128])
-        for b in range(down_blocks + up_blocks, n * lane_blocks):
-            put(b, jnp.zeros((terms.shape[1], 128), BF16))
-
-    def down_term():
+        for b in range(2):
+            put(down_blocks + 2 * j + b, term[:, b * 128 : (b + 1) * 128])
+
+    def down_term(j):
+        at = j * 256
+        term = jnp.dot(pieces[0], hidden[:, at : at + 256], preferred_element_type=F32) * product
+        term = term.astype(BF16)
+        for b in range(2):
+            put(2 * j + b, term[:, b * 128 : (b + 1) * 128])
+
+    def take_back():
         hidden_copy.wait()
         for copy in mcopies:
             copy.wait_recv()
+        for copy in mcopies:
+            copy.wait_send()
         total = pieces[0].astype(F32)
         for j in range(1, m):
             total = total + pieces[j].astype(F32)
-        term = jnp.dot(total.astype(BF16), hidden[...], preferred_element_type=F32) * product
-        term = term.astype(BF16)
-        for b in range(down_blocks):
-            put(b, term[:, b * 128 : (b + 1) * 128])
+        pieces[0] = total.astype(BF16)
+
+    def send_terms():
+        for b in range(down_blocks + up_blocks, n * lane_blocks):
+            put(b, jnp.zeros((terms.shape[1], 128), BF16))
         for d, peer in enumerate(dp_peers):
             copy = remote(
                 terms.at[peer], shares.at[me], rsend.at[d], rrecv.at[d], {"dp": peer}
@@ -381,11 +401,21 @@
             copy.start()
             fcopies.append(copy)
 
-    todo = {0: [back], 1: [up_term], 2: [down_term], 4: [sum_terms]}
+    tasks = [functools.partial(back, j) for j in range(piece_count)] + [send_back]
+    ups = [functools.partial(up_term, j) for j in range(up_blocks // 2)]
+    tasks += ups[: len(ups) // 2] + [take_back]
+    tasks += [functools.partial(down_term, j) for j in range(down_blocks // 2)]
+    tasks += ups[len(ups) // 2 :] + [send_terms]
+    begins = (n - 1) * CUTS * 5 // 7
+    after = [[] for _ in range((n - 1) * CUTS)]
+    for k, task in enumerate(tasks):
+        after[k * begins // len(tasks)].append(task)
+    after[(n - 1) * CUTS - CUTS - 1].append(sum_terms)
     for step in range(n - 1):
-        ring(step)
-        for action in todo.get(step, ()):
-            action()
+        for cut in range(CUTS):
+            ring(step, cut)
+            for task in after[step * CUTS + cut]:
+                task()
     for cut in range(CUTS):
         span = pl.ds(cut * rows, rows)
         for own, slot, out, last in (
@@ -397,14 +427,7 @@
             ).astype(BF16)
     for copy in fcopies:
         copy.wait_recv()
-    for b in range(down_blocks + up_blocks):
-        at = b % lane_blocks * 128
-        block = final[b // lane_blocks, :, at : at + 128].astype(F32)
-        if b < down_blocks:
-            down_out[:, b * 128 : (b + 1) * 128] = block
-        else:
-            up_out[:, (b - down_blocks) * 128 : (b - down_blocks + 1) * 128] = block
-    for row in kcopies + vcopies + [mcopies, rcopies, fcopies]:
+    for row in kcopies + vcopies + [rcopies, fcopies]:
         for copy in row:
             copy.wait_send()
 
@@ -423,18 +446,16 @@
         out_shape=(
             jax.ShapeDtypeStruct(block, BF16),
             jax.ShapeDtypeStruct(block, BF16),
-            jax.ShapeDtypeStruct((rank, depth), F32),
-            jax.ShapeDtypeStruct((rank, width), F32),
+            jax.ShapeDtypeStruct((n, rank, lanes), BF16),
         ),
         in_specs=[vmem] * 4 + [far] * 2,
-        out_specs=(vmem,) * 4,
+        out_specs=(vmem,) * 3,
         scratch_shapes=[
             pltpu.VMEM((tokens, depth), BF16),
             pltpu.VMEM((tokens, width), BF16),
             pltpu.VMEM((n - 1,) + block, BF16),
             pltpu.VMEM((n - 1,) + block, BF16),
             pltpu.VMEM((m, rank, tokens), BF16),
-            pltpu.VMEM((n, rank, lanes), BF16),
             pltpu.VMEM((n, rank, lanes), BF16),
             pltpu.VMEM((n, rank, lanes), BF16),
             dma((n - 1, CUTS)), dma((n - 1, CUTS)), dma((n - 1, CUTS)), dma((n - 1, CUTS)),
@@ -447,6 +468,37 @@
         ),
         name="reduce_gradients",
     )(kb, vb, inner, up, hidden, dq)
+
+
+def place_kernel(pk, pv, terms, pk_out, pv_out, down_out, up_out):
+    pk_out[0] = pk[...]
+    pv_out[0] = pv[...]
+    lane_blocks = terms.shape[2] // 128
+    down_blocks = down_out.shape[1] // 128
+    for b in range(down_blocks + up_out.shape[1] // 128):
+        at = b % lane_blocks * 128
+        block = terms[b // lane_blocks, :, at : at + 128].astype(F32)
+        if b < down_blocks:
+            down_out[:, b * 128 : (b + 1) * 128] = block
+        else:
+            up_out[:, (b - down_blocks) * 128 : (b - down_blocks + 1) * 128] = block
+
+
+def place_results(pk, pv, terms, depth, width):
+    rank = terms.shape[1]
+    vmem = pl.BlockSpec(memory_space=pltpu.VMEM)
+    return pl.pallas_call(
+        place_kernel,
+        out_shape=(
+            jax.ShapeDtypeStruct((1,) + pk.shape, BF16),
+            jax.ShapeDtypeStruct((1,) + pv.shape, BF16),
+            jax.ShapeDtypeStruct((rank, depth), F32),
+            jax.ShapeDtypeStruct((rank, width), F32),
+        ),
+        in_specs=[vmem] * 3,
+        out_specs=(vmem,) * 4,
+        name="place_results",
+    )(pk, pv, terms)
 
 
 def shards(
@@ -472,11 +524,12 @@
         response_keys, response_values, gk, gv,
     )
     product = adapter_scale / math.sqrt(hidden.shape[0] * n)
-    pk, pv, down, up = reduce(
+    pk, pv, terms = reduce(
         n, m, product, kb, vb, inner, adapter_up_factor, hidden,
         dq.reshape(-1, dq.shape[2]),
     )
-    return dq, dko, dvo, pk[None], pv[None], down.T, up
+    pk, pv, down, up = place_results(pk, pv, terms, hidden.shape[1], dq.shape[2])
+    return dq, dko, dvo, pk, pv, down.T, up
 
 
 def solution(mesh):

time: 114 us -> 108 us (0.947)
  local copies, waits for them, and re-layouts: 6.4 us -> 0 us
    unnamed x4 -> x0, local copies, waits for them, and re-layouts: 6.4 us -> none
    pallas_call x0 -> x1, Pallas kernels: none -> 1.94 us  [place_results(): pl.pallas_call(place_kernel, out_shape=(jax.ShapeDtypeStruct((1,) + pk.sh...]
where the time goes in v2:
time: 108 us
  Pallas kernels  107 us (99%)
    pallas_call x1, Pallas kernels, reduce(): pl.pallas_call(functools.partial(reduce_kernel, n, m, product), out_shape...  41.8 us
    pallas_call x1, Pallas kernels, gather(): pl.pallas_call(functools.partial(gather_kernel, n, m), out_shape=(jax.Sha...  34.5 us
    pallas_call x1, Pallas kernels, attention(): pl.pallas_call(attention_kernel, grid_spec=pltpu.PrefetchScalarGridSpec(n...  28.9 us

profile of v2, /device:TPU:0, one launch (start us, length us, event | category | flops | bytes accessed | tf_op | source)
XLA Modules:
  0.0 107.7 jit_solution(10148890208761392270)
XLA Ops:
  0.6 34.5 %gather_prompts.1 = (bf16[8,256,256]{2,1,0:T(8,128)(2,1)}, bf16[8,256,256]{2,1,0:T(8,128)(2,1)}, bf16[32,1280]{1,0:T(8,128)(2,1)}) custom-call(bf16[256,256]{1,0:T(8,128)(2,1)} %bitcast.9, bf16[256,256]{1,0:T(8,128)(2,1)} %bitcast.10, bf16[1280,1280]{1,0:T(8,128)(2,1)} %bitcast.6, bf16[32,1280]{1,0:T(8,128)(2,1)} %bitcast.11), custom_call_target="tpu_custom_call" | custom-call | tf_op jit(solution)/shard_map/gather_prompts/pallas_call | solution.py:135
  35.1 28.9 %attention_backward.1 = (bf16[16,80,2048]{2,1,0:T(8,128)(2,1)}, bf16[16,80,256]{2,1,0:T(8,128)(2,1)}, bf16[16,80,256]{2,1,0:T(8,128)(2,1)}, bf16[8,256,256]{2,1,0:T(8,128)(2,1)}, bf16[8,256,256]{2,1,0:T(8,128)(2,1)}) custom-call(s32[16]{0:T(128)} %owners.1, s32[16]{0:T(128)} %lengths.1, bf16[16,80,2048]{2,1,0:T(8,128)(2,1)} %q.1, bf16[16,80,2048]{2,1,0:T(8,128)(2,1)} %g.1, ...), custom_call_target="tpu_custom_call" | custom-call | tf_op jit(solution)/shard_map/attention_backward/pallas_call | solution.py:258
  64.0 41.8 %reduce_gradients.1 = (bf16[256,256]{1,0:T(8,128)(2,1)}, bf16[256,256]{1,0:T(8,128)(2,1)}, bf16[8,32,512]{2,1,0:T(8,128)(2,1)}) custom-call(bf16[8,256,256]{2,1,0:T(8,128)(2,1)} %get-tuple-element.27.kb, bf16[8,256,256]{2,1,0:T(8,128)(2,1)} %get-tuple-element.28.vb, bf16[32,1280]{1,0:T(8,128)(2,1)} %get-tuple-element.29.inner, bf16[32,2048]{1,0:T(8,128)(2,1)} %up.1, ...), custom_call_target="tpu_custom_call" | custom-call | tf_op jit(solution)/shard_map/reduce_gradients/pallas_call | solution.py:444
  105.8 1.9 %place_results.1 = (bf16[1,256,256]{2,1,0:T(8,128)(2,1)}, bf16[1,256,256]{2,1,0:T(8,128)(2,1)}, f32[32,1280]{1,0:T(8,128)}, f32[32,2048]{1,0:T(8,128)}) custom-call(bf16[256,256]{1,0:T(8,128)(2,1)} %get-tuple-element.30.pk, bf16[256,256]{1,0:T(8,128)(2,1)} %get-tuple-element.31.pv, bf16[8,32,512]{2,1,0:T(8,128)(2,1)} %get-tuple-element.32.terms), custom_call_target="tpu_custom_call" | custom-call | tf_op jit(solution)/shard_map/place_results/pallas_call | solution.py:490
